TPU v7x, 32 devices: a whole 2x2x4 slice. The times are simulated.
32 devices in a mesh: grp: 2 (over x), row: 4 (over y, core), col: 4 (over z).
Axes of the slice: x: 2, y: 2, z: 4, core: 2. Of those that a mesh axis runs over, the one named last changes fastest.
Arguments:
- pair: bfloat16 [128, 64, 128], P(('grp', 'row'), 'col'), parts along dimension 0, may hold values from -6 to 6
- cotangent: bfloat16 [128, 64, 128], P(('grp', 'row'), 'col'), parts along dimension 0, may hold values from -6 to 6
- token_mask: int32 [128], P('grp'), parts along dimension 0, may hold values from 0 to 1, as said below
- proj_weights: bfloat16 [4, 128, 128], replicated, may hold values from -0.5 to 0.5
- out_weights: bfloat16 [2, 128, 128], replicated, may hold values from -0.5 to 0.5
- norm_gains: float32 [2, 128], replicated, may hold values from 0.5 to 1.5
- norm_biases: float32 [2, 128], replicated, may hold values from -3 to 3
Outputs:
- grad_pair: bfloat16 [128, 64, 128], P(('grp', 'row'), 'col'), parts along dimension 0
- grad_pair_t: bfloat16 [128, 64, 128], P(('grp', 'row'), 'col'), parts along dimension 0
- grad_mats: float32 [12, 128, 128], P('grp'), parts along dimension 0
- grad_norms: float32 [8, 128], P('grp'), parts along dimension 0
There are 2 independent parts, one for each index of `grp`. A program takes and returns all parts, laid end to end along the dimension named above; an argument that names none is the same for every part. Nothing has to cross between parts.
Inputs may be any that keep to these rules, and one draw needn't show every extreme that they name: `token_mask`: 1 on a prefix of the tokens and 0 after it; at least half of the tokens and not all are 1.
All inputs are finite; a program needn't handle non-finite values.
Results may differ from a plain program's by a relative error of at most 0.012.
Values may be sent and summed in bfloat16 or wider, within the bound.
A program may use at most 128 MiB of HBM per device.

v0:
```python
import jax
import jax.numpy as jnp
from jax import lax
from jax.sharding import PartitionSpec as P

EPS = 1e-05


def spread_2(x, axis, root):
    mine = lax.axis_index(axis) == root
    return lax.psum(jnp.where(mine, x, jnp.zeros_like(x)), axis)


def plain_norm(source):
    source = source.astype(jnp.float32)
    center = source - jnp.mean(source, axis=-1, keepdims=True)
    spread = lax.rsqrt(jnp.mean(center * center, axis=-1, keepdims=True) + EPS)
    return (center * spread, spread)


def matmul(operand, weight):
    extent = operand.shape
    flattened = operand.reshape(-1, extent[-1])
    result = jnp.dot(flattened, weight, preferred_element_type=jnp.float32)
    return result.reshape(extent[:-1] + (weight.shape[-1],))


def column_sum(values):
    return jnp.sum(values.reshape(-1, values.shape[-1]), axis=0)


def outer_sum(first, second):
    return jnp.dot(
        first.reshape(-1, first.shape[-1]).T,
        second.reshape(-1, second.shape[-1]),
        preferred_element_type=jnp.float32,
    )


def project(normed, weight, gate_weight, pair_mask):
    linear = matmul(normed, weight)
    opened = jax.nn.sigmoid(matmul(normed, gate_weight))
    return ((opened * linear * pair_mask).astype(jnp.bfloat16), linear, opened)


def project_back(d_proj, normed, linear, opened, pair_mask, weight, gate_weight):
    upstream = d_proj.astype(jnp.float32) * pair_mask
    d_linear = (upstream * opened).astype(jnp.bfloat16)
    d_opened = (upstream * linear * opened * (1.0 - opened)).astype(jnp.bfloat16)
    grad_weight = outer_sum(normed, d_linear)
    grad_gate = outer_sum(normed, d_opened)
    returned = matmul(d_linear, weight.T) + matmul(d_opened, gate_weight.T)
    return (returned, grad_weight, grad_gate)


def norm_back(upstream, normal, spread, gain_vec):
    scaled_up = upstream * gain_vec
    returned = spread * (
        scaled_up
        - jnp.mean(scaled_up, axis=-1, keepdims=True)
        - normal * jnp.mean(scaled_up * normal, axis=-1, keepdims=True)
    )
    return (returned, column_sum(upstream * normal), column_sum(upstream))


def output_back(mixing, normed, cotangent, out_weight, gate_weight, gain_vec, bias_vec):
    normal, spread = plain_norm(mixing)
    ynorm = (normal * gain_vec + bias_vec).astype(jnp.bfloat16)
    outer = matmul(ynorm, out_weight)
    opened = jax.nn.sigmoid(matmul(normed, gate_weight))
    upstream = cotangent.astype(jnp.float32)
    d_out = (upstream * opened).astype(jnp.bfloat16)
    d_opened = (upstream * outer * opened * (1.0 - opened)).astype(jnp.bfloat16)
    grad_out = outer_sum(ynorm, d_out)
    grad_gate = outer_sum(normed, d_opened)
    d_norm = matmul(d_out, out_weight.T)
    d_mixing, grad_gain, grad_bias = norm_back(d_norm, normal, spread, gain_vec)
    return (
        d_mixing.astype(jnp.bfloat16),
        matmul(d_opened, gate_weight.T),
        grad_out,
        grad_gate,
        grad_gain,
        grad_bias,
    )


def take_cols(values, offset, amount):
    return lax.dynamic_slice_in_dim(values, offset, amount, 1)


def per_device(pair, cotangent, token_mask, proj_weights, out_weights, norm_gains, norm_biases):
    tile_rows = pair.shape[0]
    tile_cols = pair.shape[1]
    tokens = token_mask.shape[0]
    repeat_count = lax.axis_size("row") // lax.axis_size("col")
    row_index = lax.axis_index("row")
    col_index = lax.axis_index("col")
    presence = token_mask.astype(jnp.float32)
    row_presence = lax.dynamic_slice_in_dim(presence, row_index * tile_rows, tile_rows)
    col_presence = lax.dynamic_slice_in_dim(presence, col_index * tile_cols, tile_cols)
    tile_mask = (row_presence[:, None] * col_presence[None, :])[:, :, None]
    gain_in = norm_gains[0]
    bias_in = norm_biases[0]
    strip = lax.all_gather(pair, "col", axis=1, tiled=True)
    strip_normal, strip_spread = plain_norm(strip)
    strip_normed = (strip_normal * gain_in + bias_in).astype(jnp.bfloat16)
    strip_mask = (row_presence[:, None] * presence[None, :])[:, :, None]
    left_rows, strip_lin, strip_open = project(
        strip_normed, proj_weights[0], proj_weights[1], strip_mask
    )
    first_col = col_index * tile_cols
    normal = take_cols(strip_normal, first_col, tile_cols)
    spread = take_cols(strip_spread, first_col, tile_cols)
    normed = take_cols(strip_normed, first_col, tile_cols)
    left_lin = take_cols(strip_lin, first_col, tile_cols)
    left_open = take_cols(strip_open, first_col, tile_cols)
    first_key = row_index * tile_rows
    side_mask = (col_presence[:, None] * row_presence[None, :])[:, :, None]
    pieces = []
    for offset in range(repeat_count):
        pieces.append(spread_2(strip, "row", col_index * repeat_count + offset))
    column_pairs = jnp.concatenate(pieces, axis=0)
    right_normal, right_spread = plain_norm(column_pairs)
    right_normed = (right_normal * gain_in + bias_in).astype(jnp.bfloat16)
    right_mask = (col_presence[:, None] * presence[None, :])[:, :, None]
    right_rows, right_lin, right_open = project(
        right_normed, proj_weights[2], proj_weights[3], right_mask
    )
    side_normal = take_cols(right_normal, first_key, tile_rows)
    side_spread = take_cols(right_spread, first_key, tile_rows)
    side_normed = take_cols(right_normed, first_key, tile_rows)
    side_lin = take_cols(right_lin, first_key, tile_rows)
    side_open = take_cols(right_open, first_key, tile_rows)
    mixing = jnp.einsum("ikh,jkh->ijh", left_rows, right_rows, preferred_element_type=jnp.float32)
    d_mixing, d_gate_in, grad_out, grad_gate, grad_gain, grad_bias = output_back(
        mixing, normed, cotangent, out_weights[0], out_weights[1], norm_gains[1], norm_biases[1]
    )
    portion = take_cols(right_rows, jnp.int32(0), lax.axis_size("col") * tile_cols)
    d_left = lax.psum_scatter(
        jnp.einsum("ijh,jkh->kih", d_mixing, portion, preferred_element_type=jnp.float32).astype(
            jnp.bfloat16
        ),
        "col",
        scatter_dimension=0,
        tiled=True,
    ).astype(jnp.float32)
    d_left = jnp.transpose(d_left, (1, 0, 2)).astype(jnp.bfloat16)
    portion = take_cols(left_rows, jnp.int32(0), lax.axis_size("row") * tile_rows)
    d_right = lax.psum_scatter(
        jnp.einsum("ijh,ikh->kjh", d_mixing, portion, preferred_element_type=jnp.float32).astype(
            jnp.bfloat16
        ),
        "row",
        scatter_dimension=0,
        tiled=True,
    ).astype(jnp.float32)
    d_right = jnp.transpose(d_right, (1, 0, 2)).astype(jnp.bfloat16)
    back_left, grad_lw, grad_lg = project_back(
        d_left, normed, left_lin, left_open, tile_mask, proj_weights[0], proj_weights[1]
    )
    back_right, grad_rw, grad_rg = project_back(
        d_right, side_normed, side_lin, side_open, side_mask, proj_weights[2], proj_weights[3]
    )
    main_back, gain_main, bias_main = norm_back(back_left + d_gate_in, normal, spread, gain_in)
    side_back, gain_side, bias_side = norm_back(back_right, side_normal, side_spread, gain_in)
    matrices = jnp.stack([grad_lw, grad_lg, grad_rw, grad_rg, grad_out, grad_gate])
    vectors = jnp.stack([gain_main + gain_side, bias_main + bias_side, grad_gain, grad_bias])
    matrices, vectors = lax.psum((matrices, vectors), ("row", "col"))
    grad_pair = main_back.astype(jnp.bfloat16)
    grad_pair_t = jnp.transpose(side_back, (1, 0, 2)).astype(jnp.bfloat16)
    return (grad_pair, grad_pair_t, matrices / tokens, vectors / tokens)


def solution(mesh):
    in_specs = (
        P(("grp", "row"), "col", None),
        P(("grp", "row"), "col", None),
        P("grp"),
        P(),
        P(),
        P(),
        P(),
    )
    out_specs = (
        P(("grp", "row"), "col", None),
        P(("grp", "row"), "col", None),
        P("grp", None, None),
        P("grp", None),
    )
    return jax.shard_map(
        per_device, mesh=mesh, in_specs=in_specs, out_specs=out_specs, check_vma=False
    )
```

profile of v0, /device:TPU:0, one launch (start us, length us, event | category | flops | bytes accessed | tf_op | source)
XLA Modules:
  0.0 243.6 jit_solution(14269031472316884799)
XLA Ops:
  7.2 15.8 %all_gather.3 = bf16[16,64,128]{2,1,0:T(8,128)(2,1)S(1)} all-gather(bf16[16,16,128]{2,1,0:T(8,128)(2,1)} %param.7), channel_id=1, replica_groups=mesh['grp'=2,'row'=4,'col'=4] {'col'}, dimensions={1}, use_global_device_ids=true | all-gather | bytes 327680 | tf_op jit(solution)/shard_map/all_gather | solution.py:105
  23.1 0.7 broadcast_select_fusion
  25.0 0.6 copy-done.27
  25.7 0.6 copy-done.34
  28.0 1.1 multiply_convert_fusion
  29.9 0.8 fusion.24
  30.8 0.7 fusion.80
  31.5 0.7 div.69
  32.2 25.3 %all-reduce.3.cloned.1.call-done = bf16[16,64,128]{2,1,0:T(8,128)(2,1)} async-done(((bf16[16,64,128]{2,1,0:T(8,128)(2,1)}), bf16[16,64,128]{2,1,0:T(8,128)(2,1)}) %all-reduce.3.cloned.1.call-update) | async-done | bytes 262160 | tf_op jit(solution)/shard_map/psum | solution.py:11
  57.5 1.2 convert_reduce_fusion
  60.5 1.1 multiply_convert_fusion.1
  63.3 0.7 copy-done.25
  64.0 0.7 multiply_reduce_fusion
  64.8 0.6 copy-done.21
  66.5 1.1 copy.90
  67.7 0.6 copy-done.28
  68.4 0.7 constant_dynamic-slice_fusion.1
  69.4 1.1 copy.97
  70.8 0.7 copy-done.10
  71.9 15.6 %reduce-scatter.3.cloned.1.call-done = bf16[16,16,128]{2,0,1:T(8,128)(2,1)} async-done(((bf16[64,16,128]{2,0,1:T(8,128)(2,1)}), bf16[16,16,128]{2,0,1:T(8,128)(2,1)}) %reduce-scatter.3.cloned.1.call-update) | async-done | bytes 65552 | tf_op jit(solution)/shard_map/reduce_scatter | solution.py:140
  87.4 1.1 fusion.36
  88.9 19.2 %reduce-scatter.5.cloned.1.call-done = bf16[16,16,128]{2,0,1:T(8,128)(2,1)} async-done(((bf16[64,16,128]{2,0,1:T(8,128)(2,1)}), bf16[16,16,128]{2,0,1:T(8,128)(2,1)}) %reduce-scatter.5.cloned.1.call-update) | async-done | bytes 65552 | tf_op jit(solution)/shard_map/reduce_scatter | solution.py:150
  108.2 1.1 fusion.30
  109.5 0.6 copy-done.23
  111.6 32.5 %psum.23 = f32[4,128]{1,0:T(4,128)S(1)} all-reduce(f32[4,128]{1,0:T(4,128)S(1)} %pad_maximum_fusion), channel_id=1, replica_groups=mesh['grp'=2,'row'=4,'col'=4] {'row','col'}, use_global_device_ids=true, to_apply=%region_22.23 | all-reduce | flops 512 | bytes 4096 | tf_op jit(solution)/shard_map/psum | solution.py:169
  144.7 0.6 copy-done.19
  145.9 0.7 copy-done.7
  146.9 0.7 copy.102
  147.6 0.8 multiply_convert_fusion.3
  148.4 0.6 broadcast_multiply_fusion.13
  149.0 86.3 %all-reduce.5.cloned.1.call-done = f32[6,128,128]{2,1,0:T(8,128)} async-done(((f32[6,128,128]{2,1,0:T(8,128)}), f32[6,128,128]{2,1,0:T(8,128)}) %all-reduce.5.cloned.1.call-update) | async-done | bytes 393232 | tf_op jit(solution)/shard_map/psum | solution.py:169
  235.3 1.8 broadcast_multiply_fusion
  (136 shorter events, 12.9 us)
Async XLA Ops:
  7.2 50.3 %all-reduce.3.cloned.1.call-start = ((), (), s32[]{:S(2)}) async-start(), calls=%async_computation.2 | async-start | bytes 524288 | tf_op jit(solution)/shard_map/psum | solution.py:11
  23.8 63.6 %reduce-scatter.3.cloned.1.call-start = ((), (), s32[]{:S(2)}) async-start(), calls=%async_computation.3 | async-start | bytes 327680 | tf_op jit(solution)/shard_map/reduce_scatter | solution.py:140
  24.9 1.9 copy-start.12
  25.6 0.7 copy-start.35
  26.8 3.9 %copy-start.24 = (f32[128]{0:T(128)}, f32[128]{0:T(128)S(1)}, u32[]{:S(2)}) copy-start(f32[128]{0:T(128)S(1)} %get-tuple-element.66) | copy-start | bytes 1540
  26.8 32.3 %copy-start.22 = (f32[128]{0:T(128)}, f32[128]{0:T(128)S(1)}, u32[]{:S(2)}) copy-start(f32[128]{0:T(128)S(1)} %get-tuple-element.65) | copy-start | bytes 1540
  26.8 0.9 copy-start.8
  27.2 2.3 copy-start.1
  28.0 1.1 copy-start.5
  29.1 0.8 copy-start.9
  29.1 0.9 copy-start.16
  30.8 0.7 copy-start.18
  57.5 1.2 copy-start
  59.7 0.7 copy-start.3
  60.0 1.6 copy-start.6
  63.3 0.7 copy-start.25
  64.7 0.7 copy-start.21
  67.6 0.7 copy-start.30
  67.6 0.7 copy-start.13
  67.6 40.5 %reduce-scatter.5.cloned.1.call-start = ((), (), s32[]{:S(2)}) async-start(), calls=%async_computation.4 | async-start | bytes 327680 | tf_op jit(solution)/shard_map/reduce_scatter | solution.py:150
  69.4 1.2 copy-start.15
  70.7 0.8 copy-start.10
  70.7 0.9 copy-start.11
  70.7 0.9 copy-start.17
  70.7 164.7 %all-reduce.5.cloned.1.call-start = ((), (), s32[]{:S(2)}) async-start(), calls=%async_computation.5 | async-start | bytes 786432 | tf_op jit(solution)/shard_map/psum | solution.py:169
  70.7 0.9 copy-start.26
  70.7 0.9 copy-start.31
  71.9 16.7 %copy-start.2 = (bf16[16,64,128]{2,1,0:T(8,128)(2,1)S(1)}, bf16[16,64,128]{2,1,0:T(8,128)(2,1)}, u32[]{:S(2)}) copy-start(bf16[16,64,128]{2,1,0:T(8,128)(2,1)} %copy-done.1) | copy-start | bytes 786436
  111.3 33.0 %copy-start.4 = (bf16[16,64,128]{2,1,0:T(8,128)(2,1)S(1)}, bf16[16,64,128]{2,1,0:T(8,128)(2,1)}, u32[]{:S(2)}) copy-start(bf16[16,64,128]{2,1,0:T(8,128)(2,1)} %copy-done.3) | copy-start | bytes 786436
  144.5 0.8 copy-start.19
  145.9 0.7 copy-start.7
  146.9 0.7 copy-start.20
  (9 other events, 5.6 us)
Sparse Core Ops, SparseCore 0:
  23.9 33.5 all-reduce.2
  67.8 19.6 reduce-scatter.2
  89.9 18.2 reduce-scatter.4
  146.8 88.5 all-reduce.4
where the time goes:
time: 244 us
  waiting for transfers between devices  146 us (60%)
  blocking collectives  48.3 us (20%)
  local copies, waits for them, and re-layouts  16.1 us (7%)
  between operations  14.2 us (6%)
  other arithmetic  10.5 us (4%)
  matrix products  7.81 us (3%)
    psum x1, waiting for transfers between devices, per_device(): matrices, vectors = lax.psum((matrices, vectors), ('row', 'col'))  86.3 us
    psum x1, blocking collectives, per_device(): matrices, vectors = lax.psum((matrices, vectors), ('row', 'col'))  32.5 us
    psum x1, waiting for transfers between devices, spread_2(): return lax.psum(jnp.where(mine, x, jnp.zeros_like(x)), axis)  25.3 us
    reduce_scatter x1, waiting for transfers between devices, per_device(): lax.psum_scatter(jnp.einsum('ijh,ikh->kjh', d_mixing, portion, preferred_...  19.2 us
    all_gather x1, blocking collectives, per_device(): strip = lax.all_gather(pair, 'col', axis=1, tiled=True)  15.8 us
    reduce_scatter x1, waiting for transfers between devices, per_device(): lax.psum_scatter(jnp.einsum('ijh,jkh->kih', d_mixing, portion, preferred_...  15.6 us
    unnamed x77, local copies, waits for them, and re-layouts  9.28 us
    dot_general x12, matrix products, matmul(): result = jnp.dot(flattened, weight, preferred_element_type=jnp.float32)  5.36 us
  transfers between devices with their start and end apart: 4, of which 4 were waited for; matrix products, arithmetic and copies ran while one was open for 5% of the time, Pallas kernels for 0%

commit v1 on v0

--- a/solution.py
+++ b/solution.py
@@ -1,7 +1,15 @@
+import functools
+
 import jax
 import jax.numpy as jnp
 from jax import lax
+from jax.experimental import pallas as pl
+from jax.experimental.pallas import tpu as pltpu
 from jax.sharding import PartitionSpec as P
+
+MESH = pl.DeviceIdType.MESH
+F32 = jnp.float32
+BF16 = jnp.bfloat16
 
 EPS = 1e-05
 
@@ -172,6 +180,511 @@
     return (grad_pair, grad_pair_t, matrices / tokens, vectors / tokens)
 
 
+def dot_nt(first, second):
+    return lax.dot_general(first, second, (((1,), (1,)), ((), ())), preferred_element_type=F32)
+
+
+def dot_tn(first, second):
+    return lax.dot_general(first, second, (((0,), (0,)), ((), ())), preferred_element_type=F32)
+
+
+def dot_nn(first, second):
+    return jnp.dot(first, second, preferred_element_type=F32)
+
+
+def kernel(
+    side,
+    tile,
+    tokens,
+    mask_ref,
+    pair_ref,
+    cot_ref,
+    pw_ref,
+    ow_ref,
+    gain_ref,
+    bias_ref,
+    gp_ref,
+    gpt_ref,
+    gm_ref,
+    gn_ref,
+    lb,
+    rb,
+    sr,
+    pt,
+    lf,
+    rf,
+    dmix,
+    mix,
+    normal_s,
+    spread_s,
+    normed_s,
+    lin_s,
+    open_s,
+    gate_s,
+    mask_s,
+    tnormal_s,
+    tspread_s,
+    tnormed_s,
+    tlin_s,
+    topen_s,
+    tmask_s,
+    dgate_s,
+    tback_s,
+    sdl,
+    sdr,
+    rdl,
+    rdr,
+    early,
+    late,
+    rearly,
+    rlate,
+    aearly,
+    alate,
+    vec,
+    rvec,
+    l_send,
+    l_recv,
+    r_send,
+    r_recv,
+    p_sem,
+    dl_send,
+    dl_recv,
+    dr_send,
+    dr_recv,
+    e_send,
+    e_recv,
+    w_send,
+    w_recv,
+    ae_send,
+    ae_recv,
+    aw_send,
+    aw_recv,
+    v_send,
+    v_recv,
+):
+    r = lax.axis_index("row")
+    c = lax.axis_index("col")
+    n = side * side
+    me = r * side + c
+    cells = tile * tile
+    erows = early.shape[0] // n
+    wrows = late.shape[0] // n
+
+    def at(t):
+        return {"row": t // side, "col": lax.rem(t, side)}
+
+    def remote(src, dst, send, recv, row, col):
+        return pltpu.make_async_remote_copy(
+            src_ref=src,
+            dst_ref=dst,
+            send_sem=send,
+            recv_sem=recv,
+            device_id={"row": row, "col": col},
+            device_id_type=MESH,
+        )
+
+    def others(body):
+        def step(p, carry):
+            body(lax.rem(me + p, n))
+            return carry
+
+        lax.fori_loop(1, n, step, 0)
+
+    barrier = pltpu.get_barrier_semaphore()
+    others(
+        lambda t: pl.semaphore_signal(barrier, inc=1, device_id=at(t), device_id_type=MESH)
+    )
+
+    gain_in = gain_ref[0:1, :]
+    bias_in = bias_ref[0:1, :]
+    gain_mix = gain_ref[1:2, :]
+    bias_mix = bias_ref[1:2, :]
+
+    sub = lax.broadcasted_iota(jnp.int32, (tile, 128), 0)
+    row_vec = jnp.zeros((tile, 128), F32)
+    col_vec = jnp.zeros((tile, 128), F32)
+    row_bits = []
+    col_bits = []
+    for a in range(tile):
+        row_bits.append(mask_ref[r * tile + a].astype(F32))
+        col_bits.append(mask_ref[c * tile + a].astype(F32))
+        row_vec = jnp.where(sub == a, row_bits[a], row_vec)
+        col_vec = jnp.where(sub == a, col_bits[a], col_vec)
+    for a in range(tile):
+        mask_s[a * tile : (a + 1) * tile, :] = col_vec * row_bits[a]
+        tmask_s[a * tile : (a + 1) * tile, :] = row_vec * col_bits[a]
+
+    normal, spread = plain_norm(pair_ref[...].reshape(cells, 128))
+    normed = (normal * gain_in + bias_in).astype(BF16)
+    normal_s[...] = normal
+    spread_s[...] = jnp.broadcast_to(spread, (cells, 128))
+    normed_s[...] = normed
+    pair_mask = mask_s[...]
+    lin = dot_nn(normed, pw_ref[0])
+    opened = jax.nn.sigmoid(dot_nn(normed, pw_ref[1]))
+    lin_s[...] = lin
+    open_s[...] = opened
+    lb[c] = (opened * lin * pair_mask).astype(BF16).reshape(tile, tile, 128)
+    rlin = dot_nn(normed, pw_ref[2])
+    ropen = jax.nn.sigmoid(dot_nn(normed, pw_ref[3]))
+    sr[...] = (ropen * rlin * pair_mask).astype(BF16).reshape(tile, tile, 128)
+
+    pl.semaphore_wait(barrier, n - 1)
+
+    def left_copy(d):
+        return remote(
+            lb.at[c], lb.at[c], l_send.at[d], l_recv.at[c], r, lax.rem(c + d, side)
+        )
+
+    def right_copy(d):
+        return remote(
+            sr, rb.at[c], r_send.at[d], r_recv.at[c], lax.rem(r + d, side), r
+        )
+
+    def pair_copy():
+        return remote(pair_ref, pt, p_sem.at[0], p_sem.at[1], c, r)
+
+    def left_arrival(b):
+        return remote(lb.at[b], lb.at[b], l_send.at[0], l_recv.at[b], r, c)
+
+    def right_arrival(b):
+        return remote(sr, rb.at[b], r_send.at[0], r_recv.at[b], r, c)
+
+    for d in range(1, side):
+        left_copy(d).start()
+        right_copy(d).start()
+
+    @pl.when(r != c)
+    def _():
+        right_copy(0).start()
+        pair_copy().start()
+
+    @pl.when(r == c)
+    def _():
+        rb[c] = sr[...]
+        pt[...] = pair_ref[...]
+
+    gate_s[...] = jax.nn.sigmoid(dot_nn(normed, ow_ref[1]))
+
+    def mix_block(d, accs):
+        b = lax.rem(c + d, side)
+
+        @pl.when(d > 0)
+        def _():
+            left_arrival(b).wait_recv()
+
+        @pl.when(jnp.logical_or(d > 0, r != c))
+        def _():
+            right_arrival(b).wait_recv()
+
+        base = pl.multiple_of(b * cells, cells)
+        lf[pl.ds(base, cells), :] = lb[b].astype(F32).reshape(cells, 128)
+        rf[pl.ds(base, cells), :] = rb[b].astype(F32).reshape(cells, 128)
+
+        def step(k, accs):
+            right = rf[pl.ds(base + k, tile, stride=tile), :]
+            return tuple(
+                accs[i] + lf[pl.ds(base + i * tile + k, 1), :] * right for i in range(tile)
+            )
+
+        return lax.fori_loop(0, tile, step, accs)
+
+    zero = jnp.zeros((tile, 128), F32)
+    accs = lax.fori_loop(0, side, mix_block, (zero,) * tile)
+    for i in range(tile):
+        mix[i * tile : (i + 1) * tile, :] = accs[i]
+
+    xhat, mspread = plain_norm(mix[...])
+    ynorm = (xhat * gain_mix + bias_mix).astype(BF16)
+    upstream = cot_ref[...].reshape(cells, 128).astype(F32)
+    gate = gate_s[...]
+    d_out = (upstream * gate).astype(BF16)
+    d_norm = dot_nt(d_out, ow_ref[0])
+    scaled = d_norm * gain_mix
+    d_mixing = mspread * (
+        scaled
+        - jnp.mean(scaled, axis=-1, keepdims=True)
+        - xhat * jnp.mean(scaled * xhat, axis=-1, keepdims=True)
+    )
+    dmix[...] = d_mixing.astype(BF16).astype(F32)
+    vec[...] = jnp.zeros_like(vec)
+    vec[2:3, :] = jnp.sum(d_norm * xhat, axis=0, keepdims=True)
+    vec[3:4, :] = jnp.sum(d_norm, axis=0, keepdims=True)
+    outer = dot_nn(ynorm, ow_ref[0])
+    d_open = (upstream * outer * gate * (1.0 - gate)).astype(BF16)
+    early[0:128, :] = dot_tn(ynorm, d_out).astype(BF16)
+    early[128:256, :] = dot_tn(normed_s[...], d_open).astype(BF16)
+    dgate_s[...] = dot_nt(d_open, ow_ref[1])
+
+    def chunk_copy(src, rows, dst, send, recv, t):
+        return remote(
+            src.at[pl.ds(pl.multiple_of(t * rows, rows), rows)],
+            dst.at[me],
+            send.at[t],
+            recv.at[me],
+            t // side,
+            lax.rem(t, side),
+        )
+
+    def chunk_arrival(src, rows, dst, send, recv, t):
+        return remote(
+            src.at[pl.ds(0, rows)], dst.at[t], send.at[t], recv.at[t], r, c
+        )
+
+    others(lambda t: chunk_copy(early, erows, rearly, e_send, e_recv, t).start())
+    rearly[me] = early[pl.ds(pl.multiple_of(me * erows, erows), erows), :]
+
+    group = 4
+
+    def left_part(b, out, slot):
+        def step(g, carry):
+            first = g * group
+            sums = [zero] * group
+            for j in range(tile):
+                right = rf[pl.ds(pl.multiple_of(b * cells + j * tile, tile), tile), :]
+                for q in range(group):
+                    sums[q] = sums[q] + dmix[pl.ds((first + q) * tile + j, 1), :] * right
+            for q in range(group):
+                out[slot, first + q] = sums[q].astype(BF16)
+            return carry
+
+        lax.fori_loop(0, tile // group, step, 0)
+
+    def right_part(b, out, slot):
+        def step(g, carry):
+            first = g * group
+            sums = [zero] * group
+            for i in range(tile):
+                left = lf[pl.ds(pl.multiple_of(b * cells + i * tile, tile), tile), :]
+                for q in range(group):
+                    sums[q] = sums[q] + dmix[pl.ds(i * tile + first + q, 1), :] * left
+            for q in range(group):
+                out[slot, first + q] = sums[q].astype(BF16)
+            return carry
+
+        lax.fori_loop(0, tile // group, step, 0)
+
+    def dl_copy(b):
+        return remote(sdl.at[b], rdl.at[c], dl_send.at[b], dl_recv.at[c], r, b)
+
+    def dr_copy(b):
+        return remote(sdr.at[b], rdr.at[r], dr_send.at[b], dr_recv.at[r], b, c)
+
+    def dl_arrival(b):
+        return remote(sdl.at[b], rdl.at[b], dl_send.at[b], dl_recv.at[b], r, c)
+
+    def dr_arrival(b):
+        return remote(sdr.at[b], rdr.at[b], dr_send.at[b], dr_recv.at[b], r, c)
+
+    def part_step(d, carry):
+        b = lax.rem(c + d, side)
+        left_part(b, sdl, b)
+        dl_copy(b).start()
+        b = lax.rem(r + d, side)
+        right_part(b, sdr, b)
+        dr_copy(b).start()
+        return carry
+
+    lax.fori_loop(1, side, part_step, 0)
+    left_part(c, rdl, c)
+    right_part(r, rdr, r)
+
+    @pl.when(r != c)
+    def _():
+        pair_copy().wait_recv()
+
+    tnormal, tspread = plain_norm(pt[...].reshape(cells, 128))
+    tnormed = (tnormal * gain_in + bias_in).astype(BF16)
+    tnormal_s[...] = tnormal
+    tspread_s[...] = jnp.broadcast_to(tspread, (cells, 128))
+    tnormed_s[...] = tnormed
+    tlin_s[...] = dot_nn(tnormed, pw_ref[2])
+    topen_s[...] = jax.nn.sigmoid(dot_nn(tnormed, pw_ref[3]))
+
+    others(lambda t: chunk_arrival(early, erows, rearly, e_send, e_recv, t).wait_recv())
+    total = rearly[0].astype(F32)
+    for s in range(1, n):
+        total = total + rearly[s].astype(F32)
+    aearly[me] = (total / tokens).astype(BF16)
+
+    def all_copy(buf, send, recv, t):
+        return remote(
+            buf.at[me], buf.at[me], send.at[t], recv.at[me], t // side, lax.rem(t, side)
+        )
+
+    def all_arrival(buf, send, recv, t):
+        return remote(buf.at[t], buf.at[t], send.at[t], recv.at[t], r, c)
+
+    others(lambda t: all_copy(aearly, ae_send, ae_recv, t).start())
+
+    def branch_back(received, mask, opened, linear, normed, first):
+        total = received[0].astype(F32)
+        for s in range(1, side):
+            total = total + received[s].astype(F32)
+        up = total.astype(BF16).astype(F32).reshape(cells, 128) * mask
+        d_lin = (up * opened).astype(BF16)
+        d_gate = (up * linear * opened * (1.0 - opened)).astype(BF16)
+        late[first * 128 : (first + 1) * 128, :] = dot_tn(normed, d_lin).astype(BF16)
+        late[(first + 1) * 128 : (first + 2) * 128, :] = dot_tn(normed, d_gate).astype(BF16)
+        return dot_nt(d_lin, pw_ref[first]) + dot_nt(d_gate, pw_ref[first + 1])
+
+    for d in range(1, side):
+        dl_arrival(lax.rem(c + d, side)).wait_recv()
+    back_left = branch_back(rdl, mask_s[...], open_s[...], lin_s[...], normed_s[...], 0)
+    for d in range(1, side):
+        dr_arrival(lax.rem(r + d, side)).wait_recv()
+    back_right = branch_back(rdr, tmask_s[...], topen_s[...], tlin_s[...], tnormed_s[...], 2)
+
+    others(lambda t: chunk_copy(late, wrows, rlate, w_send, w_recv, t).start())
+    rlate[me] = late[pl.ds(pl.multiple_of(me * wrows, wrows), wrows), :]
+
+    main, gain_main, bias_main = norm_back(
+        back_left + dgate_s[...], normal_s[...], spread_s[...], gain_in
+    )
+    turned, gain_side, bias_side = norm_back(
+        back_right, tnormal_s[...], tspread_s[...], gain_in
+    )
+    vec[0:1, :] = (gain_main + gain_side)[None, :]
+    vec[1:2, :] = (bias_main + bias_side)[None, :]
+
+    def vec_copy(t):
+        return remote(
+            vec, rvec.at[me], v_send.at[t], v_recv.at[me], t // side, lax.rem(t, side)
+        )
+
+    def vec_arrival(t):
+        return remote(vec, rvec.at[t], v_send.at[t], v_recv.at[t], r, c)
+
+    others(lambda t: vec_copy(t).start())
+    rvec[me] = vec[...]
+    gp_ref[...] = main.astype(BF16).reshape(tile, tile, 128)
+    tback_s[...] = turned
+    for k in range(tile):
+        gpt_ref[k] = tback_s[pl.ds(k, tile, stride=tile), :].astype(BF16)
+
+    others(lambda t: chunk_arrival(late, wrows, rlate, w_send, w_recv, t).wait_recv())
+    total = rlate[0].astype(F32)
+    for s in range(1, n):
+        total = total + rlate[s].astype(F32)
+    alate[me] = (total / tokens).astype(BF16)
+    others(lambda t: all_copy(alate, aw_send, aw_recv, t).start())
+
+    others(lambda t: vec_arrival(t).wait_recv())
+    total = rvec[0]
+    for s in range(1, n):
+        total = total + rvec[s]
+    gn_ref[...] = total[0:4, :] / tokens
+
+    others(lambda t: all_arrival(aearly, ae_send, ae_recv, t).wait_recv())
+    gm_ref[4:6] = aearly[...].astype(F32).reshape(2, 128, 128)
+
+    for d in range(1, side):
+        left_copy(d).wait_send()
+        right_copy(d).wait_send()
+        dl_copy(lax.rem(c + d, side)).wait_send()
+        dr_copy(lax.rem(r + d, side)).wait_send()
+
+    @pl.when(r != c)
+    def _():
+        right_copy(0).wait_send()
+        pair_copy().wait_send()
+
+    def sent(t):
+        chunk_copy(early, erows, rearly, e_send, e_recv, t).wait_send()
+        chunk_copy(late, wrows, rlate, w_send, w_recv, t).wait_send()
+        all_copy(aearly, ae_send, ae_recv, t).wait_send()
+        vec_copy(t).wait_send()
+
+    others(sent)
+    others(lambda t: all_arrival(alate, aw_send, aw_recv, t).wait_recv())
+    gm_ref[0:4] = alate[...].astype(F32).reshape(4, 128, 128)
+    others(lambda t: all_copy(alate, aw_send, aw_recv, t).wait_send())
+
+
+def fused(side, pair, cotangent, token_mask, proj_weights, out_weights, norm_gains, norm_biases):
+    tile = pair.shape[0]
+    tokens = token_mask.shape[0]
+    n = side * side
+    cells = tile * tile
+    erows = 256 // n
+    wrows = 512 // n
+    block = (side, tile, tile, 128)
+    wide = pltpu.VMEM((cells, 128), F32)
+    slim = pltpu.VMEM((cells, 128), BF16)
+    dma = pltpu.SemaphoreType.DMA
+    vmem = pl.BlockSpec(memory_space=pltpu.VMEM)
+    return pl.pallas_call(
+        functools.partial(kernel, side, tile, tokens),
+        out_shape=(
+            jax.ShapeDtypeStruct((tile, tile, 128), BF16),
+            jax.ShapeDtypeStruct((tile, tile, 128), BF16),
+            jax.ShapeDtypeStruct((6, 128, 128), F32),
+            jax.ShapeDtypeStruct((4, 128), F32),
+        ),
+        in_specs=[pl.BlockSpec(memory_space=pltpu.SMEM)] + [vmem] * 6,
+        out_specs=(vmem,) * 4,
+        scratch_shapes=[
+            pltpu.VMEM(block, BF16),
+            pltpu.VMEM(block, BF16),
+            pltpu.VMEM((tile, tile, 128), BF16),
+            pltpu.VMEM((tile, tile, 128), BF16),
+            pltpu.VMEM((side * cells, 128), F32),
+            pltpu.VMEM((side * cells, 128), F32),
+            wide,
+            wide,
+            wide,
+            wide,
+            slim,
+            wide,
+            wide,
+            wide,
+            wide,
+            wide,
+            wide,
+            slim,
+            wide,
+            wide,
+            wide,
+            wide,
+            wide,
+            pltpu.VMEM(block, BF16),
+            pltpu.VMEM(block, BF16),
+            pltpu.VMEM(block, BF16),
+            pltpu.VMEM(block, BF16),
+            pltpu.VMEM((256, 128), BF16),
+            pltpu.VMEM((512, 128), BF16),
+            pltpu.VMEM((n, erows, 128), BF16),
+            pltpu.VMEM((n, wrows, 128), BF16),
+            pltpu.VMEM((n, erows, 128), BF16),
+            pltpu.VMEM((n, wrows, 128), BF16),
+            pltpu.VMEM((8, 128), F32),
+            pltpu.VMEM((n, 8, 128), F32),
+            dma((side,)),
+            dma((side,)),
+            dma((side,)),
+            dma((side,)),
+            dma((2,)),
+            dma((side,)),
+            dma((side,)),
+            dma((side,)),
+            dma((side,)),
+        ]
+        + [dma((n,))] * 10,
+        compiler_params=pltpu.CompilerParams(
+            collective_id=0, has_side_effects=True, vmem_limit_bytes=40 * 1024 * 1024
+        ),
+    )(token_mask, pair, cotangent, proj_weights, out_weights, norm_gains, norm_biases)
+
+
+def device_program(*args):
+    rows, cols = lax.axis_size("row"), lax.axis_size("col")
+    pair = args[0]
+    square = rows == cols and pair.shape[0] == pair.shape[1] == 16
+    if square and 256 % (16 * rows * cols) == 0 and pair.shape[2] == 128:
+        return fused(rows, *args)
+    return per_device(*args)
+
+
 def solution(mesh):
     in_specs = (
         P(("grp", "row"), "col", None),
@@ -189,5 +702,5 @@
         P("grp", None),
     )
     return jax.shard_map(
-        per_device, mesh=mesh, in_specs=in_specs, out_specs=out_specs, check_vma=False
-    )
+        device_program, mesh=mesh, in_specs=in_specs, out_specs=out_specs, check_vma=False
+    )

time: 244 us -> 58.2 us (0.24)
  waiting for transfers between devices: 146 us -> 0 us
  Pallas kernels: 0 us -> 49.2 us
  blocking collectives: 48.3 us -> 0 us
  between operations: 14.2 us -> 0.66 us
  other arithmetic: 10.5 us -> 0 us
  local copies, waits for them, and re-layouts: 16.1 us -> 8.01 us
  matrix products: 7.81 us -> 0 us
    psum x2 -> x0, waiting for transfers between devices: 112 us -> none  [the longest x1 86.3 us: per_device(): matrices, vectors = lax.psum((matrices, vectors), ('row', 'col'))]
    pallas_call x0 -> x1, Pallas kernels: none -> 49.2 us  [fused(): pl.pallas_call(functools.partial(kernel, side, tile, tokens), out_shape=(...]
    reduce_scatter x2 -> x0, waiting for transfers between devices: 34.8 us -> none  [the longest x1 19.2 us: per_device(): lax.psum_scatter(jnp.einsum('ijh,ikh->kjh', d_mixing, portion, preferred_...]
    psum x1 -> x0, blocking collectives: 32.5 us -> none  [per_device(): matrices, vectors = lax.psum((matrices, vectors), ('row', 'col'))]
    all_gather x1 -> x0, blocking collectives: 15.8 us -> none  [per_device(): strip = lax.all_gather(pair, 'col', axis=1, tiled=True)]
    dot_general x21 -> x0, matrix products: 7.81 us -> none  [the longest x12 5.36 us: matmul(): result = jnp.dot(flattened, weight, preferred_element_type=jnp.float32)]
    reduce_sum x7 -> x0, other arithmetic: 3.34 us -> none  [the longest x2 1.44 us: plain_norm(): center = source - jnp.mean(source, axis=-1, keepdims=True)]
    convert_element_type x5 -> x0, other arithmetic: 3.23 us -> none  [the longest x2 2.22 us: project_back(): (upstream * linear * opened * (1.0 - opened)).astype(jnp.bfloat16)]
  transfers between devices with their start and end apart: 4 -> 0, of which waited for: 4 -> 0; matrix products, arithmetic and copies ran while one was open for 5% -> 0% of each run, Pallas kernels for 0% -> 0%
where the time goes in v1:
time: 58.2 us; the launch traced here: 57.9 us
  Pallas kernels  49.2 us (85%)
  local copies, waits for them, and re-layouts  8.01 us (14%)
  between operations  0.66 us (1%)
    pallas_call x1, Pallas kernels, fused(): pl.pallas_call(functools.partial(kernel, side, tile, tokens), out_shape=(...  49.2 us
    unnamed x18, local copies, waits for them, and re-layouts  8.01 us

profile of v1, /device:TPU:0, one launch (start us, length us, event | category | flops | bytes accessed | tf_op | source)
XLA Modules:
  0.0 57.9 jit_solution(8955462034468109241)
XLA Ops:
  0.6 0.0 copy-start
  0.6 0.9 %copy-done = bf16[4,128,128]{2,1,0:T(8,128)(2,1)S(1)} copy-done((bf16[4,128,128]{2,1,0:T(8,128)(2,1)S(1)}, bf16[4,128,128]{2,1,0:T(8,128)(2,1)}, u32[]{:S(2)}) %copy-start) | copy-done | bytes 131096
  1.5 0.0 copy-start.1
  1.5 0.8 %copy-done.1 = bf16[16,16,128]{2,1,0:T(8,128)(2,1)S(1)} copy-done((bf16[16,16,128]{2,1,0:T(8,128)(2,1)S(1)}, bf16[16,16,128]{2,1,0:T(8,128)(2,1)}, u32[]{:S(2)}) %copy-start.1) | copy-done | bytes 65560
  2.4 0.0 copy-start.2
  2.4 0.8 %copy-done.2 = bf16[16,16,128]{2,1,0:T(8,128)(2,1)S(1)} copy-done((bf16[16,16,128]{2,1,0:T(8,128)(2,1)S(1)}, bf16[16,16,128]{2,1,0:T(8,128)(2,1)}, u32[]{:S(2)}) %copy-start.2) | copy-done | bytes 65560
  3.2 0.0 copy-start.3
  3.2 0.8 %copy-done.3 = bf16[2,128,128]{2,1,0:T(8,128)(2,1)S(1)} copy-done((bf16[2,128,128]{2,1,0:T(8,128)(2,1)S(1)}, bf16[2,128,128]{2,1,0:T(8,128)(2,1)}, u32[]{:S(2)}) %copy-start.3) | copy-done | bytes 65560
  4.1 0.0 copy-start.4
  4.1 0.7 %copy-done.4 = f32[2,128]{1,0:T(2,128)S(1)} copy-done((f32[2,128]{1,0:T(2,128)S(1)}, f32[2,128]{1,0:T(2,128)}, u32[]{:S(2)}) %copy-start.4) | copy-done | bytes 1048
  4.7 0.0 copy-start.5
  4.7 0.7 %copy-done.5 = f32[2,128]{1,0:T(2,128)S(1)} copy-done((f32[2,128]{1,0:T(2,128)S(1)}, f32[2,128]{1,0:T(2,128)}, u32[]{:S(2)}) %copy-start.5) | copy-done | bytes 1048
  5.4 0.0 copy-start.6
  5.4 0.7 %copy-done.6 = s32[64]{0:T(128)S(1)} copy-done((s32[64]{0:T(128)S(1)}, s32[64]{0:T(128)}, u32[]{:S(2)}) %copy-start.6) | copy-done | bytes 280
  6.1 49.2 %shard_map.102 = (bf16[16,16,128]{2,1,0:T(8,128)(2,1)S(1)}, bf16[16,16,128]{2,1,0:T(8,128)(2,1)S(1)}, f32[6,128,128]{2,1,0:T(8,128)S(1)}, f32[4,128]{1,0:T(4,128)S(1)}) custom-call(s32[64]{0:T(128)S(1)} %copy-done.6, bf16[16,16,128]{2,1,0:T(8,128)(2,1)S(1)} %copy-done.1, bf16[16,16,128]{2,1,0:T(8,128)(2,1)S(1)} %copy-done.2, ...), custom_call_target="tpu_custom_call" | custom-call | tf_op jit(solution)/shard_map/pallas_call | solution.py:616
  55.3 0.6 %copy.15 = bf16[16,16,128]{2,1,0:T(8,128)(2,1)} copy(bf16[16,16,128]{2,1,0:T(8,128)(2,1)S(1)} %get-tuple-element.8) | data formatting | bytes 131072
  55.9 0.6 %copy.16 = bf16[16,16,128]{2,1,0:T(8,128)(2,1)} copy(bf16[16,16,128]{2,1,0:T(8,128)(2,1)S(1)} %get-tuple-element.9) | data formatting | bytes 131072
  56.5 0.7 %copy.17 = f32[6,128,128]{2,1,0:T(8,128)} copy(f32[6,128,128]{2,1,0:T(8,128)S(1)} %get-tuple-element.10) | data formatting | bytes 786432
  57.3 0.6 copy.18
Async XLA Ops:
  0.6 0.9 %copy-start = (bf16[4,128,128]{2,1,0:T(8,128)(2,1)S(1)}, bf16[4,128,128]{2,1,0:T(8,128)(2,1)}, u32[]{:S(2)}) copy-start(bf16[4,128,128]{2,1,0:T(8,128)(2,1)} %pw_ref.1) | copy-start | bytes 393220
  1.5 0.8 %copy-start.1 = (bf16[16,16,128]{2,1,0:T(8,128)(2,1)S(1)}, bf16[16,16,128]{2,1,0:T(8,128)(2,1)}, u32[]{:S(2)}) copy-start(bf16[16,16,128]{2,1,0:T(8,128)(2,1)} %pair_ref.1) | copy-start | bytes 196612
  2.4 0.8 %copy-start.2 = (bf16[16,16,128]{2,1,0:T(8,128)(2,1)S(1)}, bf16[16,16,128]{2,1,0:T(8,128)(2,1)}, u32[]{:S(2)}) copy-start(bf16[16,16,128]{2,1,0:T(8,128)(2,1)} %cot_ref.1) | copy-start | bytes 196612
  3.2 0.8 %copy-start.3 = (bf16[2,128,128]{2,1,0:T(8,128)(2,1)S(1)}, bf16[2,128,128]{2,1,0:T(8,128)(2,1)}, u32[]{:S(2)}) copy-start(bf16[2,128,128]{2,1,0:T(8,128)(2,1)} %ow_ref.1) | copy-start | bytes 196612
  4.1 0.7 %copy-start.4 = (f32[2,128]{1,0:T(2,128)S(1)}, f32[2,128]{1,0:T(2,128)}, u32[]{:S(2)}) copy-start(f32[2,128]{1,0:T(2,128)} %gain_ref.1) | copy-start | bytes 3076
  4.7 0.7 %copy-start.5 = (f32[2,128]{1,0:T(2,128)S(1)}, f32[2,128]{1,0:T(2,128)}, u32[]{:S(2)}) copy-start(f32[2,128]{1,0:T(2,128)} %bias_ref.1) | copy-start | bytes 3076
  5.4 0.7 %copy-start.6 = (s32[64]{0:T(128)S(1)}, s32[64]{0:T(128)}, u32[]{:S(2)}) copy-start(s32[64]{0:T(128)} %mask_ref.1) | copy-start | bytes 772

commit v2 on v1

--- a/solution.py
+++ b/solution.py
@@ -196,6 +196,17 @@
     side,
     tile,
     tokens,
+    mask_in,
+    pair_in,
+    cot_in,
+    pw_in,
+    ow_in,
+    gain_in_ref,
+    bias_in_ref,
+    gp_ref,
+    gpt_ref,
+    gm_ref,
+    gn_ref,
     mask_ref,
     pair_ref,
     cot_ref,
@@ -203,13 +214,8 @@
     ow_ref,
     gain_ref,
     bias_ref,
-    gp_ref,
-    gpt_ref,
-    gm_ref,
-    gn_ref,
     lb,
     rb,
-    sr,
     pt,
     lf,
     rf,
@@ -242,6 +248,7 @@
     alate,
     vec,
     rvec,
+    in_sem,
     l_send,
     l_recv,
     r_send,
@@ -290,11 +297,29 @@
 
         lax.fori_loop(1, n, step, 0)
 
+    loads = [
+        pltpu.make_async_copy(src, dst, in_sem.at[at_sem])
+        for at_sem, (src, dst) in enumerate(
+            (
+                (pair_in, pair_ref),
+                (pw_in, pw_ref),
+                (mask_in, mask_ref),
+                (gain_in_ref, gain_ref),
+                (bias_in_ref, bias_ref),
+                (ow_in, ow_ref),
+                (cot_in, cot_ref),
+            )
+        )
+    ]
+    for load in loads:
+        load.start()
     barrier = pltpu.get_barrier_semaphore()
     others(
         lambda t: pl.semaphore_signal(barrier, inc=1, device_id=at(t), device_id_type=MESH)
     )
 
+    for load in loads:
+        load.wait()
     gain_in = gain_ref[0:1, :]
     bias_in = bias_ref[0:1, :]
     gain_mix = gain_ref[1:2, :]
@@ -325,9 +350,6 @@
     lin_s[...] = lin
     open_s[...] = opened
     lb[c] = (opened * lin * pair_mask).astype(BF16).reshape(tile, tile, 128)
-    rlin = dot_nn(normed, pw_ref[2])
-    ropen = jax.nn.sigmoid(dot_nn(normed, pw_ref[3]))
-    sr[...] = (ropen * rlin * pair_mask).astype(BF16).reshape(tile, tile, 128)
 
     pl.semaphore_wait(barrier, n - 1)
 
@@ -338,7 +360,7 @@
 
     def right_copy(d):
         return remote(
-            sr, rb.at[c], r_send.at[d], r_recv.at[c], lax.rem(r + d, side), r
+            rb.at[r], rb.at[r], r_send.at[d], r_recv.at[r], lax.rem(r + d, side), c
         )
 
     def pair_copy():
@@ -348,21 +370,35 @@
         return remote(lb.at[b], lb.at[b], l_send.at[0], l_recv.at[b], r, c)
 
     def right_arrival(b):
-        return remote(sr, rb.at[b], r_send.at[0], r_recv.at[b], r, c)
+        return remote(rb.at[b], rb.at[b], r_send.at[0], r_recv.at[b], r, c)
+
+    @pl.when(r != c)
+    def _():
+        pair_copy().start()
 
     for d in range(1, side):
         left_copy(d).start()
-        right_copy(d).start()
+
+    @pl.when(r == c)
+    def _():
+        pt[...] = pair_ref[...]
 
     @pl.when(r != c)
     def _():
-        right_copy(0).start()
-        pair_copy().start()
-
-    @pl.when(r == c)
-    def _():
-        rb[c] = sr[...]
-        pt[...] = pair_ref[...]
+        pair_copy().wait_recv()
+
+    tnormal, tspread = plain_norm(pt[...].reshape(cells, 128))
+    tnormed = (tnormal * gain_in + bias_in).astype(BF16)
+    tnormal_s[...] = tnormal
+    tspread_s[...] = jnp.broadcast_to(tspread, (cells, 128))
+    tnormed_s[...] = tnormed
+    tlin = dot_nn(tnormed, pw_ref[2])
+    topen = jax.nn.sigmoid(dot_nn(tnormed, pw_ref[3]))
+    tlin_s[...] = tlin
+    topen_s[...] = topen
+    rb[r] = (topen * tlin * tmask_s[...]).astype(BF16).reshape(tile, tile, 128)
+    for d in range(1, side):
+        right_copy(d).start()
 
     gate_s[...] = jax.nn.sigmoid(dot_nn(normed, ow_ref[1]))
 
@@ -373,7 +409,7 @@
         def _():
             left_arrival(b).wait_recv()
 
-        @pl.when(jnp.logical_or(d > 0, r != c))
+        @pl.when(b != r)
         def _():
             right_arrival(b).wait_recv()
 
@@ -489,18 +525,6 @@
     left_part(c, rdl, c)
     right_part(r, rdr, r)
 
-    @pl.when(r != c)
-    def _():
-        pair_copy().wait_recv()
-
-    tnormal, tspread = plain_norm(pt[...].reshape(cells, 128))
-    tnormed = (tnormal * gain_in + bias_in).astype(BF16)
-    tnormal_s[...] = tnormal
-    tspread_s[...] = jnp.broadcast_to(tspread, (cells, 128))
-    tnormed_s[...] = tnormed
-    tlin_s[...] = dot_nn(tnormed, pw_ref[2])
-    topen_s[...] = jax.nn.sigmoid(dot_nn(tnormed, pw_ref[3]))
-
     others(lambda t: chunk_arrival(early, erows, rearly, e_send, e_recv, t).wait_recv())
     total = rearly[0].astype(F32)
     for s in range(1, n):
@@ -586,7 +610,6 @@
 
     @pl.when(r != c)
     def _():
-        right_copy(0).wait_send()
         pair_copy().wait_send()
 
     def sent(t):
@@ -599,6 +622,15 @@
     others(lambda t: all_arrival(alate, aw_send, aw_recv, t).wait_recv())
     gm_ref[0:4] = alate[...].astype(F32).reshape(4, 128, 128)
     others(lambda t: all_copy(alate, aw_send, aw_recv, t).wait_send())
+
+
+def hand_over(*refs):
+    sems = refs[8]
+    copies = [pltpu.make_async_copy(refs[x], refs[x + 4], sems.at[x]) for x in range(4)]
+    for copy in copies:
+        copy.start()
+    for copy in copies:
+        copy.wait()
 
 
 def fused(side, pair, cotangent, token_mask, proj_weights, out_weights, norm_gains, norm_biases):
@@ -613,7 +645,7 @@
     slim = pltpu.VMEM((cells, 128), BF16)
     dma = pltpu.SemaphoreType.DMA
     vmem = pl.BlockSpec(memory_space=pltpu.VMEM)
-    return pl.pallas_call(
+    results = pl.pallas_call(
         functools.partial(kernel, side, tile, tokens),
         out_shape=(
             jax.ShapeDtypeStruct((tile, tile, 128), BF16),
@@ -621,12 +653,18 @@
             jax.ShapeDtypeStruct((6, 128, 128), F32),
             jax.ShapeDtypeStruct((4, 128), F32),
         ),
-        in_specs=[pl.BlockSpec(memory_space=pltpu.SMEM)] + [vmem] * 6,
+        in_specs=[pl.BlockSpec(memory_space=pl.ANY)] * 7,
         out_specs=(vmem,) * 4,
         scratch_shapes=[
+            pltpu.SMEM(token_mask.shape, jnp.int32),
+            pltpu.VMEM(pair.shape, BF16),
+            pltpu.VMEM(pair.shape, BF16),
+            pltpu.VMEM(proj_weights.shape, BF16),
+            pltpu.VMEM(out_weights.shape, BF16),
+            pltpu.VMEM(norm_gains.shape, F32),
+            pltpu.VMEM(norm_biases.shape, F32),
             pltpu.VMEM(block, BF16),
             pltpu.VMEM(block, BF16),
-            pltpu.VMEM((tile, tile, 128), BF16),
             pltpu.VMEM((tile, tile, 128), BF16),
             pltpu.VMEM((side * cells, 128), F32),
             pltpu.VMEM((side * cells, 128), F32),
@@ -659,6 +697,7 @@
             pltpu.VMEM((n, wrows, 128), BF16),
             pltpu.VMEM((8, 128), F32),
             pltpu.VMEM((n, 8, 128), F32),
+            dma((7,)),
             dma((side,)),
             dma((side,)),
             dma((side,)),
@@ -674,6 +713,14 @@
             collective_id=0, has_side_effects=True, vmem_limit_bytes=40 * 1024 * 1024
         ),
     )(token_mask, pair, cotangent, proj_weights, out_weights, norm_gains, norm_biases)
+    anywhere = pl.BlockSpec(memory_space=pl.ANY)
+    return pl.pallas_call(
+        hand_over,
+        out_shape=tuple(jax.ShapeDtypeStruct(x.shape, x.dtype) for x in results),
+        in_specs=[anywhere] * 4,
+        out_specs=(anywhere,) * 4,
+        scratch_shapes=[dma((4,))],
+    )(*results)
 
 
 def device_program(*args):

time: 58.2 us -> 68 us (1.17)
  Pallas kernels: 49.2 us -> 59 us
    pallas_call x0 -> x1, Pallas kernels: none -> 17.1 us  [fused(): pl.pallas_call(hand_over, out_shape=tuple((jax.ShapeDtypeStruct(x.shape,...]
    pallas_call x1, Pallas kernels: 49.2 us -> 42 us  [fused(): pl.pallas_call(functools.partial(kernel, side, tile, tokens), out_shape=(...]
    unnamed x18 -> x22, local copies, waits for them, and re-layouts: 8.01 us -> 7.97 us
where the time goes in v2:
time: 68 us; the launch traced here: 67.7 us
  Pallas kernels  59 us (87%)
  local copies, waits for them, and re-layouts  7.97 us (12%)
    pallas_call x1, Pallas kernels, fused(): pl.pallas_call(functools.partial(kernel, side, tile, tokens), out_shape=(...  42 us
    pallas_call x1, Pallas kernels, fused(): pl.pallas_call(hand_over, out_shape=tuple((jax.ShapeDtypeStruct(x.shape,...  17.1 us
    unnamed x22, local copies, waits for them, and re-layouts  7.97 us

profile of v2, /device:TPU:0, one launch (start us, length us, event | category | flops | bytes accessed | tf_op | source)
XLA Modules:
  0.0 67.7 jit_solution(5999494975696734663)
XLA Ops:
  0.6 0.0 copy-start.1
  0.6 0.9 %copy-done.1 = bf16[4,128,128]{2,1,0:T(8,128)(2,1)S(1)} copy-done((bf16[4,128,128]{2,1,0:T(8,128)(2,1)S(1)}, bf16[4,128,128]{2,1,0:T(8,128)(2,1)}, u32[]{:S(2)}) %copy-start.1) | copy-done | bytes 131096
  1.5 0.0 copy-start.2
  1.5 0.8 %copy-done.2 = bf16[16,16,128]{2,1,0:T(8,128)(2,1)S(1)} copy-done((bf16[16,16,128]{2,1,0:T(8,128)(2,1)S(1)}, bf16[16,16,128]{2,1,0:T(8,128)(2,1)}, u32[]{:S(2)}) %copy-start.2) | copy-done | bytes 65560
  2.4 0.0 copy-start.3
  2.4 0.8 %copy-done.3 = bf16[16,16,128]{2,1,0:T(8,128)(2,1)S(1)} copy-done((bf16[16,16,128]{2,1,0:T(8,128)(2,1)S(1)}, bf16[16,16,128]{2,1,0:T(8,128)(2,1)}, u32[]{:S(2)}) %copy-start.3) | copy-done | bytes 65560
  3.2 0.0 copy-start.4
  3.2 0.8 %copy-done.4 = bf16[2,128,128]{2,1,0:T(8,128)(2,1)S(1)} copy-done((bf16[2,128,128]{2,1,0:T(8,128)(2,1)S(1)}, bf16[2,128,128]{2,1,0:T(8,128)(2,1)}, u32[]{:S(2)}) %copy-start.4) | copy-done | bytes 65560
  4.1 0.0 copy-start.8
  4.1 0.7 %copy-done.8 = f32[2,128]{1,0:T(2,128)S(1)} copy-done((f32[2,128]{1,0:T(2,128)S(1)}, f32[2,128]{1,0:T(2,128)}, u32[]{:S(2)}) %copy-start.8) | copy-done | bytes 1048
  4.7 0.0 copy-start.9
  4.7 0.7 %copy-done.9 = f32[2,128]{1,0:T(2,128)S(1)} copy-done((f32[2,128]{1,0:T(2,128)S(1)}, f32[2,128]{1,0:T(2,128)}, u32[]{:S(2)}) %copy-start.9) | copy-done | bytes 1048
  5.4 0.0 copy-start.10
  5.4 0.7 copy-done.10
  6.1 42.0 %shard_map.102 = (bf16[16,16,128]{2,1,0:T(8,128)(2,1)S(1)}, bf16[16,16,128]{2,1,0:T(8,128)(2,1)S(1)}, f32[6,128,128]{2,1,0:T(8,128)S(1)}, f32[4,128]{1,0:T(4,128)S(1)}) custom-call(s32[64]{0:T(128)S(1)} %copy-done.10, bf16[16,16,128]{2,1,0:T(8,128)(2,1)S(1)} %copy-done.2, bf16[16,16,128]{2,1,0:T(8,128)(2,1)S(1)} %copy-done.3, ...), custom_call_target="tpu_custom_call" | custom-call | tf_op jit(solution)/shard_map/pallas_call | solution.py:648
  48.0 0.0 copy-start
  48.1 0.7 %copy-done = f32[6,128,128]{2,1,0:T(8,128)} copy-done((f32[6,128,128]{2,1,0:T(8,128)}, f32[6,128,128]{2,1,0:T(8,128)S(1)}, u32[]{:S(2)}) %copy-start) | copy-done | bytes 393240
  48.8 0.0 copy-start.5
  48.8 0.6 copy-done.5
  49.4 0.0 copy-start.6
  49.4 0.6 copy-done.6
  50.0 0.0 copy-start.7
  50.0 0.6 copy-done.7
  50.6 17.1 %shard_map.103 = (bf16[16,16,128]{2,1,0:T(8,128)(2,1)}, bf16[16,16,128]{2,1,0:T(8,128)(2,1)}, f32[6,128,128]{2,1,0:T(8,128)}, f32[4,128]{1,0:T(4,128)}) custom-call(bf16[16,16,128]{2,1,0:T(8,128)(2,1)} %copy-done.5, bf16[16,16,128]{2,1,0:T(8,128)(2,1)} %copy-done.6, f32[6,128,128]{2,1,0:T(8,128)} %copy-done, f32[4,128]{1,0:T(4,128)} %copy-done.7), custom_call_target="tpu_custom_call" | custom-call | tf_op jit(solution)/shard_map/pallas_call | solution.py:717
Async XLA Ops:
  0.6 0.9 %copy-start.1 = (bf16[4,128,128]{2,1,0:T(8,128)(2,1)S(1)}, bf16[4,128,128]{2,1,0:T(8,128)(2,1)}, u32[]{:S(2)}) copy-start(bf16[4,128,128]{2,1,0:T(8,128)(2,1)} %pw_in.1) | copy-start | bytes 393220
  1.5 0.8 %copy-start.2 = (bf16[16,16,128]{2,1,0:T(8,128)(2,1)S(1)}, bf16[16,16,128]{2,1,0:T(8,128)(2,1)}, u32[]{:S(2)}) copy-start(bf16[16,16,128]{2,1,0:T(8,128)(2,1)} %pair_in.1) | copy-start | bytes 196612
  2.4 0.8 %copy-start.3 = (bf16[16,16,128]{2,1,0:T(8,128)(2,1)S(1)}, bf16[16,16,128]{2,1,0:T(8,128)(2,1)}, u32[]{:S(2)}) copy-start(bf16[16,16,128]{2,1,0:T(8,128)(2,1)} %cot_in.1) | copy-start | bytes 196612
  3.2 0.8 %copy-start.4 = (bf16[2,128,128]{2,1,0:T(8,128)(2,1)S(1)}, bf16[2,128,128]{2,1,0:T(8,128)(2,1)}, u32[]{:S(2)}) copy-start(bf16[2,128,128]{2,1,0:T(8,128)(2,1)} %ow_in.1) | copy-start | bytes 196612
  4.1 0.7 %copy-start.8 = (f32[2,128]{1,0:T(2,128)S(1)}, f32[2,128]{1,0:T(2,128)}, u32[]{:S(2)}) copy-start(f32[2,128]{1,0:T(2,128)} %gain_in_ref.1) | copy-start | bytes 3076
  4.7 0.7 %copy-start.9 = (f32[2,128]{1,0:T(2,128)S(1)}, f32[2,128]{1,0:T(2,128)}, u32[]{:S(2)}) copy-start(f32[2,128]{1,0:T(2,128)} %bias_in_ref.1) | copy-start | bytes 3076
  5.4 0.7 copy-start.10
  48.0 0.7 %copy-start = (f32[6,128,128]{2,1,0:T(8,128)}, f32[6,128,128]{2,1,0:T(8,128)S(1)}, u32[]{:S(2)}) copy-start(f32[6,128,128]{2,1,0:T(8,128)S(1)} %get-tuple-element.10.refs_2_) | copy-start | bytes 1179652
  48.8 0.6 copy-start.5
  49.4 0.6 copy-start.6
  50.0 0.6 copy-start.7

commit v3 on v2

--- a/solution.py
+++ b/solution.py
@@ -653,7 +653,7 @@
             jax.ShapeDtypeStruct((6, 128, 128), F32),
             jax.ShapeDtypeStruct((4, 128), F32),
         ),
-        in_specs=[pl.BlockSpec(memory_space=pl.ANY)] * 7,
+        in_specs=[pl.BlockSpec(memory_space=pltpu.HBM)] * 7,
         out_specs=(vmem,) * 4,
         scratch_shapes=[
             pltpu.SMEM(token_mask.shape, jnp.int32),
@@ -710,15 +710,15 @@
         ]
         + [dma((n,))] * 10,
         compiler_params=pltpu.CompilerParams(
-            collective_id=0, has_side_effects=True, vmem_limit_bytes=40 * 1024 * 1024
+            collective_id=0, has_side_effects=True, vmem_limit_bytes=63 * 1024 * 1024
         ),
     )(token_mask, pair, cotangent, proj_weights, out_weights, norm_gains, norm_biases)
-    anywhere = pl.BlockSpec(memory_space=pl.ANY)
+    main = pl.BlockSpec(memory_space=pltpu.HBM)
     return pl.pallas_call(
         hand_over,
         out_shape=tuple(jax.ShapeDtypeStruct(x.shape, x.dtype) for x in results),
-        in_specs=[anywhere] * 4,
-        out_specs=(anywhere,) * 4,
+        in_specs=[vmem] * 4,
+        out_specs=(main,) * 4,
         scratch_shapes=[dma((4,))],
     )(*results)
 

time: 68 us -> 45.1 us (0.66)
  Pallas kernels: 59 us -> 44.3 us
  local copies, waits for them, and re-layouts: 7.97 us -> 0 us
    pallas_call x1, Pallas kernels: 17.1 us -> 1.9 us  [fused(): pl.pallas_call(hand_over, out_shape=tuple((jax.ShapeDtypeStruct(x.shape,...]
    unnamed x22 -> x0, local copies, waits for them, and re-layouts: 7.97 us -> none
where the time goes in v3:
time: 45.1 us; the launch traced here: 44.9 us
  Pallas kernels  44.3 us (98%)
  between operations  0.64 us (1%)
    pallas_call x1, Pallas kernels, fused(): pl.pallas_call(functools.partial(kernel, side, tile, tokens), out_shape=(...  42.4 us
    pallas_call x1, Pallas kernels, fused(): pl.pallas_call(hand_over, out_shape=tuple((jax.ShapeDtypeStruct(x.shape,...  1.9 us

profile of v3, /device:TPU:0, one launch (start us, length us, event | category | flops | bytes accessed | tf_op | source)
XLA Modules:
  0.0 44.9 jit_solution(2779767263083749581)
XLA Ops:
  0.6 42.4 %shard_map.102 = (bf16[16,16,128]{2,1,0:T(8,128)(2,1)}, bf16[16,16,128]{2,1,0:T(8,128)(2,1)}, f32[6,128,128]{2,1,0:T(8,128)}, f32[4,128]{1,0:T(4,128)}) custom-call(s32[64]{0:T(128)} %mask_in.1, bf16[16,16,128]{2,1,0:T(8,128)(2,1)} %pair_in.1, bf16[16,16,128]{2,1,0:T(8,128)(2,1)} %cot_in.1, bf16[4,128,128]{2,1,0:T(8,128)(2,1)} %pw_in.1, ...), custom_call_target="tpu_custom_call" | custom-call | tf_op jit(solution)/shard_map/pallas_call | solution.py:648
  43.0 1.9 %shard_map.103 = (bf16[16,16,128]{2,1,0:T(8,128)(2,1)}, bf16[16,16,128]{2,1,0:T(8,128)(2,1)}, f32[6,128,128]{2,1,0:T(8,128)}, f32[4,128]{1,0:T(4,128)}) custom-call(bf16[16,16,128]{2,1,0:T(8,128)(2,1)} %get-tuple-element.8.refs_0_, bf16[16,16,128]{2,1,0:T(8,128)(2,1)} %get-tuple-element.9.refs_1_, f32[6,128,128]{2,1,0:T(8,128)} %get-tuple-element.10.refs_2_, ...), custom_call_target="tpu_custom_call" | custom-call | tf_op jit(solution)/shard_map/pallas_call | solution.py:717

commit v4 on v3

--- a/solution.py
+++ b/solution.py
@@ -240,14 +240,15 @@
     sdr,
     rdl,
     rdr,
-    early,
-    late,
-    rearly,
-    rlate,
-    aearly,
-    alate,
+    grad,
+    rowin,
+    zpart,
+    zin,
+    whole,
     vec,
     rvec,
+    zvec,
+    cvec,
     in_sem,
     l_send,
     l_recv,
@@ -258,27 +259,24 @@
     dl_recv,
     dr_send,
     dr_recv,
-    e_send,
-    e_recv,
-    w_send,
-    w_recv,
-    ae_send,
-    ae_recv,
-    aw_send,
-    aw_recv,
-    v_send,
-    v_recv,
+    rs_send,
+    rs_recv,
+    zs_send,
+    zs_recv,
+    za_send,
+    za_recv,
+    ra_send,
+    ra_recv,
+    vr_send,
+    vr_recv,
+    vz_send,
+    vz_recv,
 ):
     r = lax.axis_index("row")
     c = lax.axis_index("col")
-    n = side * side
-    me = r * side + c
     cells = tile * tile
-    erows = early.shape[0] // n
-    wrows = late.shape[0] // n
-
-    def at(t):
-        return {"row": t // side, "col": lax.rem(t, side)}
+    rows = 256 // side
+    part = rows // side
 
     def remote(src, dst, send, recv, row, col):
         return pltpu.make_async_remote_copy(
@@ -289,13 +287,6 @@
             device_id={"row": row, "col": col},
             device_id_type=MESH,
         )
-
-    def others(body):
-        def step(p, carry):
-            body(lax.rem(me + p, n))
-            return carry
-
-        lax.fori_loop(1, n, step, 0)
 
     loads = [
         pltpu.make_async_copy(src, dst, in_sem.at[at_sem])
@@ -314,9 +305,19 @@
     for load in loads:
         load.start()
     barrier = pltpu.get_barrier_semaphore()
-    others(
-        lambda t: pl.semaphore_signal(barrier, inc=1, device_id=at(t), device_id_type=MESH)
-    )
+
+    def greet(row, col):
+        pl.semaphore_signal(
+            barrier, inc=1, device_id={"row": row, "col": col}, device_id_type=MESH
+        )
+
+    for d in range(1, side):
+        greet(lax.rem(r + d, side), c)
+        greet(r, lax.rem(c + d, side))
+
+    @pl.when(r != c)
+    def _():
+        greet(c, r)
 
     for load in loads:
         load.wait()
@@ -351,7 +352,13 @@
     open_s[...] = opened
     lb[c] = (opened * lin * pair_mask).astype(BF16).reshape(tile, tile, 128)
 
-    pl.semaphore_wait(barrier, n - 1)
+    @pl.when(r != c)
+    def _():
+        pl.semaphore_wait(barrier, 2 * side - 1)
+
+    @pl.when(r == c)
+    def _():
+        pl.semaphore_wait(barrier, 2 * side - 2)
 
     def left_copy(d):
         return remote(
@@ -446,29 +453,77 @@
     vec[...] = jnp.zeros_like(vec)
     vec[2:3, :] = jnp.sum(d_norm * xhat, axis=0, keepdims=True)
     vec[3:4, :] = jnp.sum(d_norm, axis=0, keepdims=True)
-    outer = dot_nn(ynorm, ow_ref[0])
-    d_open = (upstream * outer * gate * (1.0 - gate)).astype(BF16)
-    early[0:128, :] = dot_tn(ynorm, d_out).astype(BF16)
-    early[128:256, :] = dot_tn(normed_s[...], d_open).astype(BF16)
-    dgate_s[...] = dot_nt(d_open, ow_ref[1])
-
-    def chunk_copy(src, rows, dst, send, recv, t):
-        return remote(
-            src.at[pl.ds(pl.multiple_of(t * rows, rows), rows)],
-            dst.at[me],
-            send.at[t],
-            recv.at[me],
-            t // side,
-            lax.rem(t, side),
-        )
-
-    def chunk_arrival(src, rows, dst, send, recv, t):
-        return remote(
-            src.at[pl.ds(0, rows)], dst.at[t], send.at[t], recv.at[t], r, c
-        )
-
-    others(lambda t: chunk_copy(early, erows, rearly, e_send, e_recv, t).start())
-    rearly[me] = early[pl.ds(pl.multiple_of(me * erows, erows), erows), :]
+    sends = []
+
+    def begin(copy):
+        copy.start()
+        sends.append(copy)
+
+    def row_copy(src, dst, send, recv, base, x):
+        return remote(src, dst, send.at[base + x], recv.at[base + r], x, c)
+
+    def col_copy(src, dst, send, recv, base, y):
+        return remote(src, dst, send.at[base + y], recv.at[base + c], r, y)
+
+    def arrive(dst, recv, at_sem):
+        remote(dst, dst, recv.at[at_sem], recv.at[at_sem], r, c).wait_recv()
+
+    row_peers = [lax.rem(r + d, side) for d in range(1, side)]
+    col_peers = [lax.rem(c + d, side) for d in range(1, side)]
+
+    def chunk(t, size):
+        return pl.ds(pl.multiple_of(t * size, size), size)
+
+    def sum_of(ref, g):
+        total = ref[g, 0].astype(F32)
+        for x in range(1, side):
+            total = total + ref[g, x].astype(F32)
+        return total
+
+    def scatter_row(g):
+        for x in row_peers:
+            begin(
+                row_copy(
+                    grad.at[g, chunk(x, rows)], rowin.at[g, r], rs_send, rs_recv, g * side, x
+                )
+            )
+        rowin[g, r] = grad[g, chunk(r, rows), :]
+
+    def scatter_col(g):
+        for x in row_peers:
+            arrive(rowin.at[g, x], rs_recv, g * side + x)
+        zpart[g] = sum_of(rowin, g).astype(BF16)
+        for y in col_peers:
+            begin(
+                col_copy(
+                    zpart.at[g, chunk(y, part)], zin.at[g, c], zs_send, zs_recv, g * side, y
+                )
+            )
+        zin[g, c] = zpart[g, chunk(c, part), :]
+
+    def gather_col(g):
+        for y in col_peers:
+            arrive(zin.at[g, y], zs_recv, g * side + y)
+        whole[g, r, c] = (sum_of(zin, g) / tokens).astype(BF16)
+        for y in col_peers:
+            begin(
+                col_copy(
+                    whole.at[g, r, c], whole.at[g, r, c], za_send, za_recv, g * side, y
+                )
+            )
+
+    def gather_row(g):
+        for y in col_peers:
+            arrive(whole.at[g, r, y], za_recv, g * side + y)
+        for x in row_peers:
+            begin(
+                row_copy(whole.at[g, r], whole.at[g, r], ra_send, ra_recv, g * side, x)
+            )
+
+    def finish(g, first):
+        for x in row_peers:
+            arrive(whole.at[g, x], ra_recv, g * side + x)
+        gm_ref[first : first + 2] = whole[g].astype(F32).reshape(2, 128, 128)
 
     group = 4
 
@@ -522,45 +577,38 @@
         return carry
 
     lax.fori_loop(1, side, part_step, 0)
+    outer = dot_nn(ynorm, ow_ref[0])
+    d_open = (upstream * outer * gate * (1.0 - gate)).astype(BF16)
+    grad[0, 0:128, :] = dot_tn(ynorm, d_out).astype(BF16)
+    grad[0, 128:256, :] = dot_tn(normed_s[...], d_open).astype(BF16)
+    dgate_s[...] = dot_nt(d_open, ow_ref[1])
+
+    scatter_row(0)
     left_part(c, rdl, c)
     right_part(r, rdr, r)
 
-    others(lambda t: chunk_arrival(early, erows, rearly, e_send, e_recv, t).wait_recv())
-    total = rearly[0].astype(F32)
-    for s in range(1, n):
-        total = total + rearly[s].astype(F32)
-    aearly[me] = (total / tokens).astype(BF16)
-
-    def all_copy(buf, send, recv, t):
-        return remote(
-            buf.at[me], buf.at[me], send.at[t], recv.at[me], t // side, lax.rem(t, side)
-        )
-
-    def all_arrival(buf, send, recv, t):
-        return remote(buf.at[t], buf.at[t], send.at[t], recv.at[t], r, c)
-
-    others(lambda t: all_copy(aearly, ae_send, ae_recv, t).start())
-
-    def branch_back(received, mask, opened, linear, normed, first):
+    def branch_back(received, mask, opened, linear, normed, first, g):
         total = received[0].astype(F32)
         for s in range(1, side):
             total = total + received[s].astype(F32)
         up = total.astype(BF16).astype(F32).reshape(cells, 128) * mask
         d_lin = (up * opened).astype(BF16)
         d_gate = (up * linear * opened * (1.0 - opened)).astype(BF16)
-        late[first * 128 : (first + 1) * 128, :] = dot_tn(normed, d_lin).astype(BF16)
-        late[(first + 1) * 128 : (first + 2) * 128, :] = dot_tn(normed, d_gate).astype(BF16)
+        grad[g, 0:128, :] = dot_tn(normed, d_lin).astype(BF16)
+        grad[g, 128:256, :] = dot_tn(normed, d_gate).astype(BF16)
         return dot_nt(d_lin, pw_ref[first]) + dot_nt(d_gate, pw_ref[first + 1])
 
+    for d in range(1, side):
+        dr_arrival(lax.rem(r + d, side)).wait_recv()
+    back_right = branch_back(rdr, tmask_s[...], topen_s[...], tlin_s[...], tnormed_s[...], 2, 1)
+    scatter_row(1)
+    scatter_col(0)
     for d in range(1, side):
         dl_arrival(lax.rem(c + d, side)).wait_recv()
-    back_left = branch_back(rdl, mask_s[...], open_s[...], lin_s[...], normed_s[...], 0)
-    for d in range(1, side):
-        dr_arrival(lax.rem(r + d, side)).wait_recv()
-    back_right = branch_back(rdr, tmask_s[...], topen_s[...], tlin_s[...], tnormed_s[...], 2)
-
-    others(lambda t: chunk_copy(late, wrows, rlate, w_send, w_recv, t).start())
-    rlate[me] = late[pl.ds(pl.multiple_of(me * wrows, wrows), wrows), :]
+    back_left = branch_back(rdl, mask_s[...], open_s[...], lin_s[...], normed_s[...], 0, 2)
+    scatter_row(2)
+    scatter_col(1)
+    gather_col(0)
 
     main, gain_main, bias_main = norm_back(
         back_left + dgate_s[...], normal_s[...], spread_s[...], gain_in
@@ -570,37 +618,31 @@
     )
     vec[0:1, :] = (gain_main + gain_side)[None, :]
     vec[1:2, :] = (bias_main + bias_side)[None, :]
-
-    def vec_copy(t):
-        return remote(
-            vec, rvec.at[me], v_send.at[t], v_recv.at[me], t // side, lax.rem(t, side)
-        )
-
-    def vec_arrival(t):
-        return remote(vec, rvec.at[t], v_send.at[t], v_recv.at[t], r, c)
-
-    others(lambda t: vec_copy(t).start())
-    rvec[me] = vec[...]
+    for x in row_peers:
+        begin(row_copy(vec, rvec.at[0, r], vr_send, vr_recv, 0, x))
+    rvec[0, r] = vec[...]
+
+    scatter_col(2)
+    gather_col(1)
+    gather_row(0)
     gp_ref[...] = main.astype(BF16).reshape(tile, tile, 128)
     tback_s[...] = turned
     for k in range(tile):
         gpt_ref[k] = tback_s[pl.ds(k, tile, stride=tile), :].astype(BF16)
 
-    others(lambda t: chunk_arrival(late, wrows, rlate, w_send, w_recv, t).wait_recv())
-    total = rlate[0].astype(F32)
-    for s in range(1, n):
-        total = total + rlate[s].astype(F32)
-    alate[me] = (total / tokens).astype(BF16)
-    others(lambda t: all_copy(alate, aw_send, aw_recv, t).start())
-
-    others(lambda t: vec_arrival(t).wait_recv())
-    total = rvec[0]
-    for s in range(1, n):
-        total = total + rvec[s]
-    gn_ref[...] = total[0:4, :] / tokens
-
-    others(lambda t: all_arrival(aearly, ae_send, ae_recv, t).wait_recv())
-    gm_ref[4:6] = aearly[...].astype(F32).reshape(2, 128, 128)
+    for x in row_peers:
+        arrive(rvec.at[0, x], vr_recv, x)
+    zvec[...] = sum_of(rvec, 0)
+    for y in col_peers:
+        begin(col_copy(zvec, cvec.at[0, c], vz_send, vz_recv, 0, y))
+    cvec[0, c] = zvec[...]
+
+    gather_col(2)
+    gather_row(1)
+    gather_row(2)
+    for y in col_peers:
+        arrive(cvec.at[0, y], vz_recv, y)
+    gn_ref[...] = sum_of(cvec, 0)[0:4, :] / tokens
 
     for d in range(1, side):
         left_copy(d).wait_send()
@@ -612,16 +654,11 @@
     def _():
         pair_copy().wait_send()
 
-    def sent(t):
-        chunk_copy(early, erows, rearly, e_send, e_recv, t).wait_send()
-        chunk_copy(late, wrows, rlate, w_send, w_recv, t).wait_send()
-        all_copy(aearly, ae_send, ae_recv, t).wait_send()
-        vec_copy(t).wait_send()
-
-    others(sent)
-    others(lambda t: all_arrival(alate, aw_send, aw_recv, t).wait_recv())
-    gm_ref[0:4] = alate[...].astype(F32).reshape(4, 128, 128)
-    others(lambda t: all_copy(alate, aw_send, aw_recv, t).wait_send())
+    finish(0, 4)
+    finish(1, 2)
+    finish(2, 0)
+    for copy in sends:
+        copy.wait_send()
 
 
 def hand_over(*refs):
@@ -636,10 +673,9 @@
 def fused(side, pair, cotangent, token_mask, proj_weights, out_weights, norm_gains, norm_biases):
     tile = pair.shape[0]
     tokens = token_mask.shape[0]
-    n = side * side
     cells = tile * tile
-    erows = 256 // n
-    wrows = 512 // n
+    rows = 256 // side
+    part = rows // side
     block = (side, tile, tile, 128)
     wide = pltpu.VMEM((cells, 128), F32)
     slim = pltpu.VMEM((cells, 128), BF16)
@@ -689,14 +725,15 @@
             pltpu.VMEM(block, BF16),
             pltpu.VMEM(block, BF16),
             pltpu.VMEM(block, BF16),
-            pltpu.VMEM((256, 128), BF16),
-            pltpu.VMEM((512, 128), BF16),
-            pltpu.VMEM((n, erows, 128), BF16),
-            pltpu.VMEM((n, wrows, 128), BF16),
-            pltpu.VMEM((n, erows, 128), BF16),
-            pltpu.VMEM((n, wrows, 128), BF16),
+            pltpu.VMEM((3, 256, 128), BF16),
+            pltpu.VMEM((3, side, rows, 128), BF16),
+            pltpu.VMEM((3, rows, 128), BF16),
+            pltpu.VMEM((3, side, part, 128), BF16),
+            pltpu.VMEM((3, side, side, part, 128), BF16),
             pltpu.VMEM((8, 128), F32),
-            pltpu.VMEM((n, 8, 128), F32),
+            pltpu.VMEM((1, side, 8, 128), F32),
+            pltpu.VMEM((8, 128), F32),
+            pltpu.VMEM((1, side, 8, 128), F32),
             dma((7,)),
             dma((side,)),
             dma((side,)),
@@ -708,7 +745,8 @@
             dma((side,)),
             dma((side,)),
         ]
-        + [dma((n,))] * 10,
+        + [dma((3 * side,))] * 8
+        + [dma((side,))] * 4,
         compiler_params=pltpu.CompilerParams(
             collective_id=0, has_side_effects=True, vmem_limit_bytes=63 * 1024 * 1024
         ),

time: 45.1 us -> 42.3 us (0.938)
  Pallas kernels: 44.3 us -> 41.5 us
    pallas_call x1, Pallas kernels: 42.4 us -> 39.6 us  [fused(): pl.pallas_call(functools.partial(kernel, side, tile, tokens), out_shape=(...]
where the time goes in v4:
time: 42.3 us; the launch traced here: 42.2 us
  Pallas kernels  41.5 us (98%)
  between operations  0.64 us (2%)
    pallas_call x1, Pallas kernels, fused(): pl.pallas_call(functools.partial(kernel, side, tile, tokens), out_shape=(...  39.6 us
    pallas_call x1, Pallas kernels, fused(): pl.pallas_call(hand_over, out_shape=tuple((jax.ShapeDtypeStruct(x.shape,...  1.9 us

profile of v4, /device:TPU:0, one launch (start us, length us, event | category | flops | bytes accessed | tf_op | source)
XLA Modules:
  0.0 42.2 jit_solution(204132676138656176)
XLA Ops:
  0.6 39.6 %shard_map.102 = (bf16[16,16,128]{2,1,0:T(8,128)(2,1)}, bf16[16,16,128]{2,1,0:T(8,128)(2,1)}, f32[6,128,128]{2,1,0:T(8,128)}, f32[4,128]{1,0:T(4,128)}) custom-call(s32[64]{0:T(128)} %mask_in.1, bf16[16,16,128]{2,1,0:T(8,128)(2,1)} %pair_in.1, bf16[16,16,128]{2,1,0:T(8,128)(2,1)} %cot_in.1, bf16[4,128,128]{2,1,0:T(8,128)(2,1)} %pw_in.1, ...), custom_call_target="tpu_custom_call" | custom-call | tf_op jit(solution)/shard_map/pallas_call | solution.py:684
  40.3 1.9 %shard_map.103 = (bf16[16,16,128]{2,1,0:T(8,128)(2,1)}, bf16[16,16,128]{2,1,0:T(8,128)(2,1)}, f32[6,128,128]{2,1,0:T(8,128)}, f32[4,128]{1,0:T(4,128)}) custom-call(bf16[16,16,128]{2,1,0:T(8,128)(2,1)} %get-tuple-element.8.refs_0_, bf16[16,16,128]{2,1,0:T(8,128)(2,1)} %get-tuple-element.9.refs_1_, f32[6,128,128]{2,1,0:T(8,128)} %get-tuple-element.10.refs_2_, ...), custom_call_target="tpu_custom_call" | custom-call | tf_op jit(solution)/shard_map/pallas_call | solution.py:755

commit v5 on v4

--- a/solution.py
+++ b/solution.py
@@ -263,8 +263,6 @@
     rs_recv,
     zs_send,
     zs_recv,
-    za_send,
-    za_recv,
     ra_send,
     ra_recv,
     vr_send,
@@ -276,7 +274,6 @@
     c = lax.axis_index("col")
     cells = tile * tile
     rows = 256 // side
-    part = rows // side
 
     def remote(src, dst, send, recv, row, col):
         return pltpu.make_async_remote_copy(
@@ -494,27 +491,15 @@
             arrive(rowin.at[g, x], rs_recv, g * side + x)
         zpart[g] = sum_of(rowin, g).astype(BF16)
         for y in col_peers:
-            begin(
-                col_copy(
-                    zpart.at[g, chunk(y, part)], zin.at[g, c], zs_send, zs_recv, g * side, y
-                )
-            )
-        zin[g, c] = zpart[g, chunk(c, part), :]
+            begin(col_copy(zpart.at[g], zin.at[g, c], zs_send, zs_recv, g * side, y))
+        zin[g, c] = zpart[g]
 
     def gather_col(g):
         for y in col_peers:
             arrive(zin.at[g, y], zs_recv, g * side + y)
-        whole[g, r, c] = (sum_of(zin, g) / tokens).astype(BF16)
-        for y in col_peers:
-            begin(
-                col_copy(
-                    whole.at[g, r, c], whole.at[g, r, c], za_send, za_recv, g * side, y
-                )
-            )
+        whole[g, r] = (sum_of(zin, g) / tokens).astype(BF16)
 
     def gather_row(g):
-        for y in col_peers:
-            arrive(whole.at[g, r, y], za_recv, g * side + y)
         for x in row_peers:
             begin(
                 row_copy(whole.at[g, r], whole.at[g, r], ra_send, ra_recv, g * side, x)
@@ -609,6 +594,7 @@
     scatter_row(2)
     scatter_col(1)
     gather_col(0)
+    gather_row(0)
 
     main, gain_main, bias_main = norm_back(
         back_left + dgate_s[...], normal_s[...], spread_s[...], gain_in
@@ -624,7 +610,7 @@
 
     scatter_col(2)
     gather_col(1)
-    gather_row(0)
+    gather_row(1)
     gp_ref[...] = main.astype(BF16).reshape(tile, tile, 128)
     tback_s[...] = turned
     for k in range(tile):
@@ -638,7 +624,6 @@
     cvec[0, c] = zvec[...]
 
     gather_col(2)
-    gather_row(1)
     gather_row(2)
     for y in col_peers:
         arrive(cvec.at[0, y], vz_recv, y)
@@ -675,7 +660,6 @@
     tokens = token_mask.shape[0]
     cells = tile * tile
     rows = 256 // side
-    part = rows // side
     block = (side, tile, tile, 128)
     wide = pltpu.VMEM((cells, 128), F32)
     slim = pltpu.VMEM((cells, 128), BF16)
@@ -728,8 +712,8 @@
             pltpu.VMEM((3, 256, 128), BF16),
             pltpu.VMEM((3, side, rows, 128), BF16),
             pltpu.VMEM((3, rows, 128), BF16),
-            pltpu.VMEM((3, side, part, 128), BF16),
-            pltpu.VMEM((3, side, side, part, 128), BF16),
+            pltpu.VMEM((3, side, rows, 128), BF16),
+            pltpu.VMEM((3, side, rows, 128), BF16),
             pltpu.VMEM((8, 128), F32),
             pltpu.VMEM((1, side, 8, 128), F32),
             pltpu.VMEM((8, 128), F32),
@@ -745,7 +729,7 @@
             dma((side,)),
             dma((side,)),
         ]
-        + [dma((3 * side,))] * 8
+        + [dma((3 * side,))] * 6
         + [dma((side,))] * 4,
         compiler_params=pltpu.CompilerParams(
             collective_id=0, has_side_effects=True, vmem_limit_bytes=63 * 1024 * 1024
@@ -765,7 +749,7 @@
     rows, cols = lax.axis_size("row"), lax.axis_size("col")
     pair = args[0]
     square = rows == cols and pair.shape[0] == pair.shape[1] == 16
-    if square and 256 % (16 * rows * cols) == 0 and pair.shape[2] == 128:
+    if square and 256 % (16 * rows) == 0 and pair.shape[2] == 128:
         return fused(rows, *args)
     return per_device(*args)
 

time: 42.3 us -> 40.2 us (0.950)
  Pallas kernels: 41.5 us -> 39.4 us
    pallas_call x1, Pallas kernels: 39.6 us -> 37.5 us  [fused(): pl.pallas_call(functools.partial(kernel, side, tile, tokens), out_shape=(...]
where the time goes in v5:
time: 40.2 us; the launch traced here: 40 us
  Pallas kernels  39.4 us (98%)
  between operations  0.64 us (2%)
    pallas_call x1, Pallas kernels, fused(): pl.pallas_call(functools.partial(kernel, side, tile, tokens), out_shape=(...  37.5 us
    pallas_call x1, Pallas kernels, fused(): pl.pallas_call(hand_over, out_shape=tuple((jax.ShapeDtypeStruct(x.shape,...  1.9 us

profile of v5, /device:TPU:0, one launch (start us, length us, event | category | flops | bytes accessed | tf_op | source)
XLA Modules:
  0.0 40.0 jit_solution(9898439707469459837)
XLA Ops:
  0.6 37.5 %shard_map.102 = (bf16[16,16,128]{2,1,0:T(8,128)(2,1)}, bf16[16,16,128]{2,1,0:T(8,128)(2,1)}, f32[6,128,128]{2,1,0:T(8,128)}, f32[4,128]{1,0:T(4,128)}) custom-call(s32[64]{0:T(128)} %mask_in.1, bf16[16,16,128]{2,1,0:T(8,128)(2,1)} %pair_in.1, bf16[16,16,128]{2,1,0:T(8,128)(2,1)} %cot_in.1, bf16[4,128,128]{2,1,0:T(8,128)(2,1)} %pw_in.1, ...), custom_call_target="tpu_custom_call" | custom-call | tf_op jit(solution)/shard_map/pallas_call | solution.py:668
  38.1 1.9 %shard_map.103 = (bf16[16,16,128]{2,1,0:T(8,128)(2,1)}, bf16[16,16,128]{2,1,0:T(8,128)(2,1)}, f32[6,128,128]{2,1,0:T(8,128)}, f32[4,128]{1,0:T(4,128)}) custom-call(bf16[16,16,128]{2,1,0:T(8,128)(2,1)} %get-tuple-element.8.refs_0_, bf16[16,16,128]{2,1,0:T(8,128)(2,1)} %get-tuple-element.9.refs_1_, f32[6,128,128]{2,1,0:T(8,128)} %get-tuple-element.10.refs_2_, ...), custom_call_target="tpu_custom_call" | custom-call | tf_op jit(solution)/shard_map/pallas_call | solution.py:739
